TPU v7x, 512 devices: a whole 4x4x16 slice. The times are simulated.
512 devices in a mesh: dp: 64 (over y, z), mp: 8 (over x, core).
Axes of the slice: x: 4, y: 4, z: 16, core: 2. Of those that a mesh axis runs over, the one named last changes fastest.
Arguments:
- hidden: bfloat16 [8192, 28672], P('dp', 'mp'), may hold values from -6 to 6
- cotangent: bfloat16 [8192, 8192], P('dp', 'mp'), may hold values from -6 to 6
- adapter_down: bfloat16 [28672, 64], P('mp'), may hold values from -0.03125 to 0.03125
- adapter_up: bfloat16 [64, 8192], P(None, 'mp'), may hold values from -0.75 to 0.75
- owner_per_block: int32 [8, 9], replicated, may hold values from 0 to 63, as said below
- left_statistics: float32 [128, 512, 512], P('dp'), as said below
- right_statistics: float32 [128, 64, 64], P('dp'), as said below
Outputs:
- update_a: bfloat16 [28672, 64], P('mp')
- update_b: bfloat16 [64, 8192], P(None, 'mp')
Inputs may be any that keep to these rules, and one draw needn't show every extreme that they name: `owner_per_block`: entry [m, b] is the dp index that owns block b of model group m; over all groups together no index owns more than 2 blocks, and some index owns exactly 2. `left_statistics`: each [s] is a symmetric positive definite matrix, the statistic of the block that dp index s // 2 holds in its slot s % 2; slots that hold no block are not read. `right_statistics`: each [s] is a symmetric positive definite matrix, ordered as left_statistics.
All inputs are finite; a program needn't handle non-finite values.
Results may differ from a plain program's by a relative error of at most 0.0052.
Values may be sent and summed in bfloat16 or wider, within the bound.
A program may use at most 64 MiB of HBM per device.

v0:
```python
import jax
import jax.numpy as jnp
from jax import lax
from jax.sharding import PartitionSpec as P

ITERS = 2


ADAPTER_SCALE = 2.0
BETA_STAT = 0.9
EPS_NORM = 1e-06


def matmul_high(first, second):
    return jnp.matmul(first, second, precision=lax.Precision.HIGHEST)


def inverse_root(stat):
    matrix_size = stat.shape[-1]
    identity = jnp.eye(matrix_size, dtype=jnp.float32)
    frobenius = jnp.sqrt(jnp.sum(stat * stat, axis=(-2, -1), keepdims=True))
    z_scale = 5.0 / (2.0 * frobenius)
    mat_m = z_scale * stat
    mat_h = jnp.sqrt(jnp.sqrt(z_scale)) * identity
    for iteration in range(ITERS):
        mat_q = (5.0 * identity - mat_m) / 4.0
        mat_h = matmul_high(mat_h, mat_q)
        if iteration + 1 < ITERS:
            square = matmul_high(mat_q, mat_q)
            mat_m = matmul_high(matmul_high(square, square), mat_m)
    return mat_h


def precondition(block, left_prev, right_prev):
    block_t = jnp.swapaxes(block, -1, -2)
    left_stat = BETA_STAT * left_prev + (1.0 - BETA_STAT) * matmul_high(block, block_t)
    right_stat = BETA_STAT * right_prev + (1.0 - BETA_STAT) * matmul_high(block_t, block)
    precond = matmul_high(matmul_high(inverse_root(left_stat), block), inverse_root(right_stat))
    mean_square = jnp.mean(precond * precond, axis=(-2, -1), keepdims=True)
    return precond * lax.rsqrt(mean_square + EPS_NORM)


def shards(
    hidden, cotangent, adapter_down, adapter_up, owner_per_block, left_statistics, right_statistics
):
    inner_piece = jnp.dot(hidden, adapter_down, preferred_element_type=jnp.float32)
    outer_part = lax.dot_general(
        cotangent, adapter_up, (((1,), (1,)), ((), ())), preferred_element_type=jnp.float32
    )
    inner_sum, outer_sum = lax.psum((inner_piece, outer_part), "mp")
    inner_product = inner_sum.astype(jnp.bfloat16)
    outer_product = outer_sum.astype(jnp.bfloat16)
    scale_factor = ADAPTER_SCALE / (hidden.shape[0] * lax.axis_size("dp"))
    grad_a = (
        lax.dot_general(
            hidden, outer_product, (((0,), (0,)), ((), ())), preferred_element_type=jnp.float32
        )
        * scale_factor
    )
    grad_b = (
        lax.dot_general(
            cotangent, inner_product, (((0,), (0,)), ((), ())), preferred_element_type=jnp.float32
        )
        * scale_factor
    )
    partial_gradient = jnp.concatenate([grad_a, grad_b], axis=0)
    reduced_sum = lax.psum(partial_gradient, "dp")
    count_of_blocks = owner_per_block.shape[1]
    capacity = left_statistics.shape[0]
    width_of_block = left_statistics.shape[1]
    adapter_rank_size = partial_gradient.shape[1]
    block_list = reduced_sum.reshape(count_of_blocks, width_of_block, adapter_rank_size)
    owners_flat = owner_per_block.reshape(-1)
    total_blocks = owners_flat.shape[0]
    same_owner = owners_flat[:, None] == owners_flat[None, :]
    earlier = jnp.arange(total_blocks)[None, :] < jnp.arange(total_blocks)[:, None]
    slot_flat = jnp.sum((same_owner & earlier).astype(jnp.int32), axis=1)
    group_start = lax.axis_index("mp") * count_of_blocks
    owners = lax.dynamic_slice_in_dim(owners_flat, group_start, count_of_blocks)
    slot_of = lax.dynamic_slice_in_dim(slot_flat, group_start, count_of_blocks)
    my_index = lax.axis_index("dp")
    chosen = (
        (owners[None, :] == my_index) & (slot_of[None, :] == jnp.arange(capacity)[:, None])
    ).astype(jnp.float32)
    my_blocks = jnp.einsum("cn,nbr->cbr", chosen, block_list, precision=lax.Precision.HIGHEST)
    update = precondition(my_blocks, left_statistics, right_statistics)
    placed = jnp.einsum("cn,cbr->nbr", chosen, update, precision=lax.Precision.HIGHEST)
    final_output = lax.psum(placed, "dp").astype(jnp.bfloat16)
    final_output = final_output.reshape(count_of_blocks * width_of_block, adapter_rank_size)
    row_count = hidden.shape[1]
    return (final_output[:row_count], final_output[row_count:].T)


def solution(mesh):
    return jax.shard_map(
        shards,
        mesh=mesh,
        in_specs=(
            P("dp", "mp"),
            P("dp", "mp"),
            P("mp", None),
            P(None, "mp"),
            P(),
            P("dp", None, None),
            P("dp", None, None),
        ),
        out_specs=(P("mp", None), P(None, "mp")),
        check_vma=False,
    )
```

profile of v0, /device:TPU:2, one launch (start us, length us, event | category | flops | bytes accessed | tf_op | source)
XLA Modules:
  0.0 658.4 jit_solution(3395895185699745339)
XLA Ops:
  7.2 1.3 fusion.61
  8.5 1.4 fusion.62
  10.0 26.4 %all-reduce = (bf16[128,64]{0,1:T(8,128)(2,1)S(1)}, bf16[128,64]{0,1:T(8,128)(2,1)S(1)}) all-reduce(f32[128,64]{0,1:T(8,128)S(1)} %fusion.62, f32[128,64]{0,1:T(8,128)S(1)} %fusion.61), channel_id=1, replica_groups=mesh['dp'=64,'mp'=8] {'mp'}, use_global_device_ids=true, to_apply=%region_2.0 | all-reduce | flops 16384 | bytes 98304 | tf_op jit(solution)/shard_map/psum | solution.py:50
  36.4 0.3 fusion
  36.6 0.2 fusion.9
  36.9 1.6 reshape.81
  38.6 0.2 convert_reduce_fusion
  39.0 0.1 fusion.22
  39.1 0.1 fusion.23
  39.2 279.4 %all-reduce.4.cloned.1.call-done = f32[9,512,64]{1,0,2:T(8,128)} async-done(((f32[9,512,64]{1,0,2:T(8,128)}), f32[9,512,64]{1,0,2:T(8,128)}) %all-reduce.4.cloned.1.call-update) | async-done | bytes 1179664 | tf_op jit(solution)/shard_map/psum | solution.py:67
  318.6 2.5 fusion.50
  321.1 0.5 multiply_reduce_fusion.2
  321.6 0.3 fusion.34
  321.9 0.2 fusion.64
  322.1 0.3 fusion.10
  322.4 2.3 multiply_reduce_fusion
  324.7 4.0 fusion.8
  328.7 3.5 fusion.63
  332.3 3.9 fusion.6
  336.2 3.9 fusion.4
  340.0 3.7 fusion.1
  343.7 2.2 fusion.28
  345.9 0.3 fusion.31
  346.2 0.3 fusion.65
  346.4 0.5 multiply_reduce_fusion.1
  346.9 0.1 broadcast_multiply_fusion
  347.0 1.1 fusion.25
  348.2 299.3 %all-reduce.5 = bf16[9,512,64]{1,0,2:T(8,128)(2,1)} all-reduce(f32[9,512,64]{1,0,2:T(8,128)S(1)} %fusion.25), channel_id=1, replica_groups=mesh['dp'=64,'mp'=8] {'dp'}, use_global_device_ids=true, to_apply=%region_7.0 | all-reduce | flops 294912 | bytes 1769472 | tf_op jit(solution)/shard_map/psum | solution.py:88
  647.4 1.1 slice.16
  648.5 1.4 slice.17
  649.9 0.9 copy.27
  650.9 0.7 copy.28
  (21 shorter events, 0.5 us)
Async XLA Ops:
  7.2 1.4 copy-start
  7.2 29.5 %copy-start.2 = (bf16[128,1024]{1,0:T(8,128)(2,1)S(1)}, bf16[128,1024]{1,0:T(8,128)(2,1)}, u32[]{:S(2)}) copy-start(bf16[128,1024]{1,0:T(8,128)(2,1)} %param.8) | copy-start | bytes 786436
  7.2 311.4 %all-reduce.4.cloned.1.call-start = ((), (), s32[]{:S(2)}) async-start(), calls=%async_computation | async-start | bytes 4194304 | tf_op jit(solution)/shard_map/psum | solution.py:67
  36.9 1.6 copy-start.4
  39.0 282.2 %copy-start.3 = (f32[2,64,64]{2,1,0:T(8,128)S(1)}, f32[2,64,64]{2,1,0:T(8,128)}, u32[]{:S(2)}) copy-start(f32[2,64,64]{2,1,0:T(8,128)} %param.13) | copy-start | bytes 98308
  318.6 3.8 copy-start.1
Sparse Core Ops, SparseCore 0:
  38.6 279.8 all-reduce.3
where the time goes:
time: 659 us; the launch traced here: 658 us
  blocking collectives  326 us (49%)
  waiting for transfers between devices  279 us (42%)
  matrix products  32.5 us (5%)
  between operations  14.3 us (2%)
    psum x1, blocking collectives, shards(): final_output = lax.psum(placed, 'dp').astype(jnp.bfloat16)  299 us
    psum x1, waiting for transfers between devices, shards(): reduced_sum = lax.psum(partial_gradient, 'dp')  279 us
    psum x1, blocking collectives, shards(): inner_sum, outer_sum = lax.psum((inner_piece, outer_part), 'mp')  26.4 us
    dot_general x14, matrix products, matmul_high(): return jnp.matmul(first, second, precision=lax.Precision.HIGHEST)  25.7 us
  transfers between devices with their start and end apart: 1, of which 1 were waited for; matrix products, arithmetic and copies ran while one was open for 0% of the time, Pallas kernels for 0%

commit v1 on v0

v1 whole, which is shorter than its diff:
```python
import functools

import jax
import jax.numpy as jnp
from jax import lax
from jax.experimental import pallas as pl
from jax.experimental.pallas import tpu as pltpu
from jax.sharding import PartitionSpec as P

Z_EXTENT = 16
BLOCKS_PER_CHUNK = 4
LANES = 128

ADAPTER_SCALE = 2.0
BETA_STAT = 0.9
EPS_NORM = 1e-06
MESH = pl.DeviceIdType.MESH
BF16 = jnp.bfloat16
F32 = jnp.float32

NN = (((1,), (0,)), ((), ()))
NT = (((1,), (1,)), ((), ()))
TN = (((0,), (0,)), ((), ()))


def split(value):
    high = value.astype(BF16)
    return high, (value - high.astype(F32)).astype(BF16)


def dot3(first, second, dims):
    (fh, fl), (sh, sl) = first, second
    dot = functools.partial(lax.dot_general, dimension_numbers=dims, preferred_element_type=F32)
    return dot(fh, sh) + (dot(fl, sh) + dot(fh, sl))


def eye(n):
    return (
        lax.broadcasted_iota(jnp.int32, (n, n), 0) == lax.broadcasted_iota(jnp.int32, (n, n), 1)
    ).astype(F32)


def total(value):
    return jnp.sum(jnp.sum(value, axis=0, keepdims=True), axis=1, keepdims=True)


def precondition(block_t, left_prev, right_prev):
    rank = block_t.shape[0]
    halves = split(block_t)
    left = BETA_STAT * left_prev + (1.0 - BETA_STAT) * dot3(halves, halves, TN)
    right = BETA_STAT * right_prev + (1.0 - BETA_STAT) * dot3(halves, halves, NT)

    left_z = 5.0 / (2.0 * jnp.sqrt(total(left * left)))
    left_s = split(left)
    right_z = 5.0 / (2.0 * jnp.sqrt(total(right * right)))
    right_m = right_z * right
    right_s = split(right_m)

    def by_left(value):
        return dot3(split(value), left_s, NN) * left_z

    def by_right(value):
        return dot3(right_s, split(value), NN)

    moved = by_left(block_t)
    for _ in range(4):
        moved = (5.0 * moved - by_left(moved)) / 4.0
    out = (5.0 * block_t - moved) / 4.0
    out = jnp.sqrt(jnp.sqrt(left_z)) * ((5.0 * out - by_left(out)) / 4.0)

    moved = right_m
    for _ in range(4):
        moved = (5.0 * moved - by_right(moved)) / 4.0
    root = (5.0 * eye(rank) - moved) / 4.0
    root = jnp.sqrt(jnp.sqrt(right_z)) * ((5.0 * root - by_right(root)) / 4.0)

    out = dot3(split(root), split(out), NN)
    mean_square = total(out * out) / (out.shape[0] * out.shape[1])
    return out * lax.rsqrt(mean_square + EPS_NORM)


def kernel(
    cfg,
    tab, hid, cot, down, up, left_hbm, right_prev,
    out_a, out_b,
    part, a_recv, io, gsend, yrecv, zstage, zsend, zrecv, grow, mpbuf, dsend, drecv, left_buf,
    fsend, frecv, fb, fmp, fmpf, hrow, fin, finf,
    left_sem, s_a1, r_a1, s_a2, r_a2, s_y, r_y, s_z, r_z, s_d1, r_d1, s_d2, r_d2,
    s_f1, r_f1, s_f2, r_f2, s_fz, r_fz, s_fy, r_fy,
):
    n_dp, n_mp, ny, nz, rank, width, nb = cfg
    parts = width // LANES
    owners = n_dp // n_mp
    cap = 2
    tile = BLOCKS_PER_CHUNK * parts
    chunks = -(-nb // BLOCKS_PER_CHUNK)
    sizes = [min(BLOCKS_PER_CHUNK, nb - c * BLOCKS_PER_CHUNK) for c in range(chunks)]
    tok = hid.shape[0]
    share = tok // n_mp
    slab = cap * parts
    rows_z = rank // ny
    blocks_a = hid.shape[1] // width

    dp = lax.axis_index("dp")
    mp = lax.axis_index("mp")
    y, z = dp // nz, lax.rem(dp, nz)
    active = lax.rem(dp, n_mp) == mp
    my_k = dp // n_mp

    def mp_peer(d):
        return lax.rem(mp + d, n_mp)

    def y_peer(d):
        return lax.rem(y + d, ny) * nz + z

    def z_of(d):
        return lax.rem(z + d, nz)

    def dp_peer(d):
        return lax.rem(dp + d, n_dp)

    def send(src, dst, ssem, rsem, **device):
        pltpu.make_async_remote_copy(
            src_ref=src, dst_ref=dst, send_sem=ssem, recv_sem=rsem,
            device_id=device, device_id_type=MESH,
        ).start()

    def drain(ref, sem):
        pltpu.make_async_copy(ref, ref, sem).wait()

    def loop(lower, upper, body):
        def step(i, carry):
            body(i)
            return carry
        lax.fori_loop(lower, upper, step, 0)

    barrier = pltpu.get_barrier_semaphore()

    def greet(**device):
        pl.semaphore_signal(barrier, inc=1, device_id=device, device_id_type=MESH)

    loop(1, n_mp, lambda d: greet(mp=mp_peer(d)))
    loop(1, ny, lambda d: greet(dp=y_peer(d)))
    loop(1, nz, lambda d: greet(dp=y * nz + z_of(d)))

    def greet_owner(k):
        owner = k * n_mp + mp

        @pl.when(owner != dp)
        def _():
            greet(dp=owner)

    loop(0, owners, greet_owner)

    @pl.when(active)
    def _():
        loop(1, n_dp, lambda d: greet(dp=dp_peer(d)))
        pltpu.make_async_copy(left_hbm, left_buf, left_sem).start()

    part[:, :rank] = jnp.dot(hid[...], down[...], preferred_element_type=F32)
    part[:, rank:2 * rank] = lax.dot_general(cot[...], up[...], NT, preferred_element_type=F32)

    common = (n_mp - 1) + (ny - 1) + (nz - 1) + owners
    pl.semaphore_wait(barrier, jnp.where(active, common - 1 + n_dp - 1, common))

    def rows(ref, index, count):
        return ref.at[pl.ds(pl.multiple_of(index * count, count), count)]

    loop(1, n_mp, lambda d: send(
        rows(part, mp_peer(d), share), a_recv.at[d - 1], s_a1, r_a1, mp=mp_peer(d)))
    drain(a_recv, r_a1)
    acc = part[pl.ds(pl.multiple_of(mp * share, share), share), :]
    for d in range(n_mp - 1):
        acc = acc + a_recv[d]
    io[mp] = acc.astype(BF16)
    loop(1, n_mp, lambda d: send(io.at[mp], io.at[mp], s_a2, r_a2, mp=mp_peer(d)))
    drain(a_recv.at[pl.ds(0, n_mp - 1)], s_a1)
    drain(io.at[pl.ds(0, n_mp - 1)], r_a2)
    both = io[...].reshape(tok, 2 * rank).astype(F32).T.astype(BF16)
    inner_t, outer_t = both[:rank], both[rank:]

    for c in range(chunks):
        for i in range(sizes[c]):
            b = c * BLOCKS_PER_CHUNK + i
            if b < blocks_a:
                piece = jnp.dot(outer_t, hid[:, b * width:(b + 1) * width], preferred_element_type=F32)
            else:
                at = (b - blocks_a) * width
                piece = jnp.dot(inner_t, cot[:, at:at + width], preferred_element_type=F32)
            gsend[:, :, b * width:(b + 1) * width] = piece.astype(BF16).reshape(ny, rows_z, width)
        span = pl.ds(c * BLOCKS_PER_CHUNK * width, sizes[c] * width)
        loop(1, ny, lambda d: send(
            gsend.at[lax.rem(y + d, ny), :, span], yrecv.at[d - 1, :, span],
            s_y.at[c], r_y.at[c], dp=y_peer(d)))

    scale = ADAPTER_SCALE / (tok * n_dp)
    for c in range(chunks):
        lo, hi = c * BLOCKS_PER_CHUNK * width, (c * BLOCKS_PER_CHUNK + sizes[c]) * width
        drain(yrecv.at[:, :, pl.ds(lo, hi - lo)], r_y.at[c])
        acc = gsend[y, :, lo:hi].astype(F32)
        for d in range(ny - 1):
            acc = acc + yrecv[d, :, lo:hi].astype(F32)
        count = sizes[c] * parts
        for t in range(tile):
            if t < count:
                zstage[c, pl.ds(t, nz, stride=tile), :] = acc[:, t * LANES:(t + 1) * LANES]
            else:
                zstage[c, pl.ds(t, nz, stride=tile), :] = jnp.zeros((nz, LANES), F32)
        zsend[c] = zstage[c].reshape(nz, tile, LANES).astype(BF16)
        loop(1, nz, lambda d: send(
            zsend.at[c, z_of(d)], zrecv.at[c, d - 1], s_z.at[c], r_z.at[c], dp=y * nz + z_of(d)))
    for c in range(chunks):
        drain(zrecv.at[c], r_z.at[c])
        acc = zstage[c, pl.ds(pl.multiple_of(z * tile, tile), tile), :]
        acc = acc + jnp.sum(zrecv[c].astype(F32), axis=0)
        grow[c * tile:(c + 1) * tile] = acc * scale

    keep = mpbuf.shape[1]
    mpbuf[mp] = grow[:keep]
    loop(1, n_mp, lambda d: send(
        grow.at[pl.ds(0, keep)], mpbuf.at[mp], s_d1, r_d1, mp=mp_peer(d)))
    drain(mpbuf.at[pl.ds(0, n_mp - 1)], r_d1)
    slots = n_dp * cap
    for k in range(owners):
        for s in range(cap):
            entry = (k * n_mp + mp) * cap + s
            group, row = tab[entry], tab[slots + entry]
            dsend[k, s * parts:(s + 1) * parts] = mpbuf[group, pl.ds(row, parts), :]

    def to_owner(k):
        owner = k * n_mp + mp

        @pl.when(owner != dp)
        def _():
            send(dsend.at[k], rows(drecv, dp, slab), s_d2, r_d2, dp=owner)

    loop(0, owners, to_owner)

    @pl.when(active)
    def _():
        drecv[pl.ds(pl.multiple_of(dp * slab, slab), slab), :] = dsend[my_k]
        drain(drecv.at[pl.ds(0, (n_dp - 1) * slab)], r_d2)
        pltpu.make_async_copy(left_hbm, left_buf, left_sem).wait()
        for s in range(cap):
            block_t = jnp.concatenate(
                [drecv[pl.ds(s * parts + p, n_dp, stride=slab), :] for p in range(parts)], axis=1)
            result = precondition(block_t, left_buf[s], right_prev[s])
            for p in range(parts):
                fsend[pl.ds(s * parts + p, n_dp, stride=slab), :] = result[:, p * LANES:(p + 1) * LANES]
        loop(1, n_dp, lambda d: send(
            rows(fsend, dp_peer(d), slab), rows(frecv, my_k, slab), s_f1, r_f1, dp=dp_peer(d)))
        frecv[pl.ds(pl.multiple_of(my_k * slab, slab), slab), :] = fsend[
            pl.ds(pl.multiple_of(dp * slab, slab), slab), :]
        drain(frecv.at[pl.ds(0, (owners - 1) * slab)], r_f1)

    @pl.when(jnp.logical_not(active))
    def _():
        drain(frecv, r_f1)

    fb[...] = frecv[...].astype(BF16)
    fmp[mp] = fb[...]
    loop(1, n_mp, lambda d: send(fb, fmp.at[mp], s_f2, r_f2, mp=mp_peer(d)))
    drain(fmp.at[pl.ds(0, n_mp - 1)], r_f2)
    fmpf[...] = fmp[...].astype(F32).reshape(fmpf.shape)
    hrow[...] = jnp.zeros(hrow.shape, F32)
    for b in range(nb):
        row = tab[2 * slots + mp * nb + b]
        hrow[b * parts:(b + 1) * parts] = fmpf[pl.ds(row, parts), :]
    for c in range(chunks):
        fin[c, y, z] = hrow[c * tile:(c + 1) * tile].astype(BF16)
    for c in range(chunks):
        loop(1, nz, lambda d: send(
            fin.at[c, y, z], fin.at[c, y, z], s_fz.at[c], r_fz.at[c], dp=y * nz + z_of(d)))
    for c in range(chunks):
        drain(fin.at[c, 0, pl.ds(0, nz - 1)], r_fz.at[c])
        loop(1, ny, lambda d: send(
            fin.at[c, y], fin.at[c, y], s_fy.at[c], r_fy.at[c], dp=y_peer(d)))
    for c in range(chunks):
        drain(fin.at[c, pl.ds(0, ny - 1)], r_fy.at[c])
        finf[...] = fin[c].astype(F32).reshape(finf.shape)
        for t in range(sizes[c] * parts):
            at = c * tile + t
            piece = finf[pl.ds(t, rank, stride=tile), :]
            if at < blocks_a * parts:
                out_a[at * LANES:(at + 1) * LANES, :] = piece.T.astype(BF16)
            else:
                at -= blocks_a * parts
                out_b[:, at * LANES:(at + 1) * LANES] = piece.astype(BF16)

    drain(io.at[pl.ds(0, n_mp - 1)], s_a2)
    for c in range(chunks):
        lo, hi = c * BLOCKS_PER_CHUNK * width, (c * BLOCKS_PER_CHUNK + sizes[c]) * width
        drain(yrecv.at[:, :, pl.ds(lo, hi - lo)], s_y.at[c])
        drain(zrecv.at[c], s_z.at[c])
        drain(fin.at[c, 0, pl.ds(0, nz - 1)], s_fz.at[c])
        drain(fin.at[c, pl.ds(0, ny - 1)], s_fy.at[c])
    drain(mpbuf.at[pl.ds(0, n_mp - 1)], s_d1)
    drain(fmp.at[pl.ds(0, n_mp - 1)], s_f2)

    @pl.when(active)
    def _():
        drain(dsend.at[pl.ds(0, owners - 1)], s_d2)
        drain(fsend.at[pl.ds(0, (n_dp - 1) * slab)], s_f1)

    @pl.when(jnp.logical_not(active))
    def _():
        drain(dsend, s_d2)


def shards(
    hidden, cotangent, adapter_down, adapter_up, owner_per_block, left_statistics, right_statistics
):
    n_dp, n_mp = lax.axis_size("dp"), lax.axis_size("mp")
    nz = Z_EXTENT
    ny = n_dp // nz
    tok, units = hidden.shape
    features = cotangent.shape[1]
    rank = adapter_down.shape[1]
    nb = owner_per_block.shape[1]
    cap, width = left_statistics.shape[:2]
    parts = width // LANES
    owners = n_dp // n_mp
    tile = BLOCKS_PER_CHUNK * parts
    chunks = -(-nb // BLOCKS_PER_CHUNK)
    slab = cap * parts
    share = tok // n_mp
    keep = -(-nb * parts // 8) * 8

    flat = owner_per_block.reshape(-1)
    count = flat.shape[0]
    order = jnp.arange(count)
    same = (flat[:, None] == flat[None, :]) & (order[None, :] < order[:, None])
    slot = jnp.sum(same.astype(jnp.int32), axis=1)
    hit = (flat * cap + slot)[None, :] == jnp.arange(n_dp * cap)[:, None]
    which = jnp.sum(jnp.where(hit, order[None, :], 0), axis=1).astype(jnp.int32)
    place = lax.rem(flat, n_mp) * (owners * slab) + (flat // n_mp) * slab + slot * parts
    table = jnp.concatenate([which // nb, lax.rem(which, nb) * parts, place]).astype(jnp.int32)

    vmem = pl.BlockSpec(memory_space=pltpu.VMEM)
    dma = pltpu.SemaphoreType.DMA
    cfg = (n_dp, n_mp, ny, nz, rank, width, nb)
    return pl.pallas_call(
        functools.partial(kernel, cfg),
        out_shape=(
            jax.ShapeDtypeStruct((units, rank), BF16),
            jax.ShapeDtypeStruct((rank, features), BF16),
        ),
        in_specs=[pl.BlockSpec(memory_space=pltpu.SMEM)] + [vmem] * 4
        + [pl.BlockSpec(memory_space=pl.ANY), vmem],
        out_specs=(vmem, vmem),
        scratch_shapes=[
            pltpu.VMEM((tok, 2 * rank), F32),
            pltpu.VMEM((n_mp - 1, share, 2 * rank), F32),
            pltpu.VMEM((n_mp, share, 2 * rank), BF16),
            pltpu.VMEM((ny, rank // ny, nb * width), BF16),
            pltpu.VMEM((ny - 1, rank // ny, nb * width), BF16),
            pltpu.VMEM((chunks, nz * tile, LANES), F32),
            pltpu.VMEM((chunks, nz, tile, LANES), BF16),
            pltpu.VMEM((chunks, nz - 1, tile, LANES), BF16),
            pltpu.VMEM((chunks * tile, LANES), F32),
            pltpu.VMEM((n_mp, keep, LANES), F32),
            pltpu.VMEM((owners, slab, LANES), F32),
            pltpu.VMEM((n_dp * slab, LANES), F32),
            pltpu.VMEM((cap, width, width), F32),
            pltpu.VMEM((n_dp * slab, LANES), F32),
            pltpu.VMEM((owners * slab, LANES), F32),
            pltpu.VMEM((owners * slab, LANES), BF16),
            pltpu.VMEM((n_mp, owners * slab, LANES), BF16),
            pltpu.VMEM((n_mp * owners * slab, LANES), F32),
            pltpu.VMEM((chunks * tile, LANES), F32),
            pltpu.VMEM((chunks, ny, nz, tile, LANES), BF16),
            pltpu.VMEM((rank * tile, LANES), F32),
            dma, dma, dma, dma, dma,
            dma((chunks,)), dma((chunks,)), dma((chunks,)), dma((chunks,)),
            dma, dma, dma, dma, dma, dma, dma, dma,
            dma((chunks,)), dma((chunks,)), dma((chunks,)), dma((chunks,)),
        ],
        compiler_params=pltpu.CompilerParams(
            collective_id=0, has_side_effects=True, vmem_limit_bytes=48 * 1024 * 1024
        ),
    )(table, hidden, cotangent, adapter_down, adapter_up, left_statistics, right_statistics)


def solution(mesh):
    return jax.shard_map(
        shards,
        mesh=mesh,
        in_specs=(
            P("dp", "mp"),
            P("dp", "mp"),
            P("mp", None),
            P(None, "mp"),
            P(),
            P("dp", None, None),
            P("dp", None, None),
        ),
        out_specs=(P("mp", None), P(None, "mp")),
        check_vma=False,
    )
```

time: 659 us -> 109 us (0.17)
  the two profiles are of different devices: /device:TPU:2 before, /device:TPU:1 now
where the time goes in v1:
time: 109 us; the launch traced here: 108 us
  Pallas kernels  97.6 us (90%)
  local copies, waits for them, and re-layouts  9.39 us (9%)
    pallas_call x1, Pallas kernels, shards(): pl.pallas_call(functools.partial(kernel, cfg), out_shape=(jax.ShapeDtypeS...  97.6 us
    unnamed x12, local copies, waits for them, and re-layouts  7.56 us

profile of v1, /device:TPU:1, one launch (start us, length us, event | category | flops | bytes accessed | tf_op | source)
XLA Modules:
  0.0 107.9 jit_solution(8602842913738117904)
XLA Ops:
  0.6 0.8 reshape.17
  1.4 0.2 convert_reduce_fusion
  1.6 0.1 select_reduce_fusion
  1.7 1.4 %copy.11.down = bf16[3584,64]{1,0:T(8,128)(2,1)S(1)} copy(bf16[3584,64]{0,1:T(8,128)(2,1)} %param.9) | data formatting | bytes 917504 | tf_op args[2]
  3.2 0.0 copy-start
  3.2 1.6 %copy-done = f32[2,512,512]{2,1,0:T(8,128)S(1)} copy-done((f32[2,512,512]{2,1,0:T(8,128)S(1)}, f32[2,512,512]{2,1,0:T(8,128)}, u32[]{:S(2)}) %copy-start) | copy-done | bytes 2097176
  4.8 0.0 copy-start.1
  4.8 1.2 %copy-done.1 = bf16[128,3584]{1,0:T(8,128)(2,1)S(1)} copy-done((bf16[128,3584]{1,0:T(8,128)(2,1)S(1)}, bf16[128,3584]{1,0:T(8,128)(2,1)}, u32[]{:S(2)}) %copy-start.1) | copy-done | bytes 917528
  6.0 0.0 copy-start.2
  6.0 0.9 copy-done.2
  6.9 0.0 copy-start.3
  6.9 0.9 copy-done.3
  7.8 0.0 copy-start.4
  7.8 0.8 copy-done.4
  8.6 97.6 %shard_map.86 = (bf16[3584,64]{1,0:T(8,128)(2,1)S(1)}, bf16[64,1024]{1,0:T(8,128)(2,1)S(1)}) custom-call(s32[328]{0:T(512)S(1)} %pad_add_fusion.tab, bf16[128,3584]{1,0:T(8,128)(2,1)S(1)} %copy-done.1, bf16[128,1024]{1,0:T(8,128)(2,1)S(1)} %copy-done.2, bf16[3584,64]{1,0:T(8,128)(2,1)S(1)} %copy.11.down, bf16[64,1024]{1,0:T(8,128)(2,1)S(1)} %copy-done.3, ...), custom_call_target="tpu_custom_call" | custom-call | tf_op jit(solution)/shard_map/pallas_call | solution.py:342
  106.2 1.1 copy.12
  107.3 0.7 copy.14
  (3 shorter events, 0.0 us)
Async XLA Ops:
  3.2 1.6 %copy-start = (f32[2,512,512]{2,1,0:T(8,128)S(1)}, f32[2,512,512]{2,1,0:T(8,128)}, u32[]{:S(2)}) copy-start(f32[2,512,512]{2,1,0:T(8,128)} %left_hbm.1) | copy-start | bytes 6291460
  4.8 1.2 %copy-start.1 = (bf16[128,3584]{1,0:T(8,128)(2,1)S(1)}, bf16[128,3584]{1,0:T(8,128)(2,1)}, u32[]{:S(2)}) copy-start(bf16[128,3584]{1,0:T(8,128)(2,1)} %hid.1) | copy-start | bytes 2752516
  6.0 0.9 copy-start.2
  6.9 0.9 copy-start.3
  7.8 0.8 copy-start.4

commit v2 on v1

v2 whole, which is shorter than its diff:
```python
import functools

import jax
import jax.numpy as jnp
from jax import lax
from jax.experimental import pallas as pl
from jax.experimental.pallas import tpu as pltpu
from jax.sharding import PartitionSpec as P

Z_EXTENT = 16
BLOCKS_PER_CHUNK = 4
LANES = 128

ADAPTER_SCALE = 2.0
BETA_STAT = 0.9
EPS_NORM = 1e-06
MESH = pl.DeviceIdType.MESH
BF16 = jnp.bfloat16
F32 = jnp.float32

NN = (((1,), (0,)), ((), ()))
NT = (((1,), (1,)), ((), ()))
TN = (((0,), (0,)), ((), ()))


def split(value):
    high = value.astype(BF16)
    return high, (value - high.astype(F32)).astype(BF16)


def dot3(first, second, dims):
    (fh, fl), (sh, sl) = split(first), split(second)
    return dot1(fh, sh, dims) + (dot1(fl, sh, dims) + dot1(fh, sl, dims))


def dot1(first, second, dims):
    return lax.dot_general(
        first.astype(BF16), second.astype(BF16), dims, preferred_element_type=F32)


def eye(n):
    return (
        lax.broadcasted_iota(jnp.int32, (n, n), 0) == lax.broadcasted_iota(jnp.int32, (n, n), 1)
    ).astype(F32)


def total(value):
    return jnp.sum(jnp.sum(value, axis=0, keepdims=True), axis=1, keepdims=True)


def precondition(blocks, lefts, rights):
    rank, width = blocks[0].shape
    n = range(len(blocks))
    lefts = [BETA_STAT * lefts[i] + (1.0 - BETA_STAT) * dot1(blocks[i], blocks[i], TN) for i in n]
    rights = [BETA_STAT * rights[i] + (1.0 - BETA_STAT) * dot1(blocks[i], blocks[i], NT) for i in n]
    short = [v.astype(BF16) for v in lefts]
    left_z = [5.0 / (2.0 * jnp.sqrt(total(v * v))) for v in lefts]
    right_z = [5.0 / (2.0 * jnp.sqrt(total(v * v))) for v in rights]
    right_m = [right_z[i] * rights[i] for i in n]

    moved = [dot1(blocks[i], short[i], NN) * left_z[i] for i in n]
    small = right_m
    for _ in range(4):
        moved = [(5.0 * moved[i] - dot1(moved[i], short[i], NN) * left_z[i]) / 4.0 for i in n]
        small = [(5.0 * small[i] - dot1(right_m[i], small[i], NN)) / 4.0 for i in n]
    outs = [(5.0 * blocks[i] - moved[i]) / 4.0 for i in n]
    roots = [(5.0 * eye(rank) - small[i]) / 4.0 for i in n]
    outs = [(5.0 * outs[i] - dot1(outs[i], short[i], NN) * left_z[i]) / 4.0 for i in n]
    roots = [(5.0 * roots[i] - dot1(right_m[i], roots[i], NN)) / 4.0 for i in n]
    gains = [jnp.sqrt(jnp.sqrt(left_z[i])) * jnp.sqrt(jnp.sqrt(right_z[i])) for i in n]
    outs = [dot3(roots[i], outs[i], NN) * gains[i] for i in n]
    return [v * lax.rsqrt(total(v * v) / (rank * width) + EPS_NORM) for v in outs]


def kernel(
    cfg,
    owner_ref, hid_hbm, cot_hbm, down_hbm, up_hbm, left_hbm, right_hbm,
    out_a, out_b,
    hid, cot, down, up, right_prev, left_buf, pbuf, gsend, yrecv, zstage, zsend, zrecv,
    rstage, rsend, rrecv, grow, mpbuf, dsend, drecv, fsend, frecv, fb, fmp, fmpf, hrow,
    fin, finr, finf, finrf, ystage,
    in_sem, left_sem, s_a, r_a, s_y, r_y, s_z, r_z, s_d1, r_d1, s_d2, r_d2,
    s_f1, r_f1, s_f2, r_f2, s_fz, r_fz, s_fy, r_fy, own_sem,
):
    n_dp, n_mp, ny, nz, rank, width, nb, cap = cfg
    parts = width // LANES
    owners = n_dp // n_mp
    tile = BLOCKS_PER_CHUNK * parts
    whole = nb // BLOCKS_PER_CHUNK
    chunks = whole + 1
    rest = (nb - whole * BLOCKS_PER_CHUNK) * parts
    sizes = [tile] * whole + [rest]
    tok, units = hid.shape
    slab = cap * parts
    rows_y = rank // ny
    blocks_a = units // width

    dp = lax.axis_index("dp")
    mp = lax.axis_index("mp")
    y, z = dp // nz, lax.rem(dp, nz)
    active = lax.rem(dp, n_mp) == mp
    my_k = dp // n_mp

    def mp_peer(d):
        return lax.rem(mp + d, n_mp)

    def y_of(d):
        return lax.rem(y + d, ny)

    def z_of(d):
        return lax.rem(z + d, nz)

    def far_first(d):
        half = nz // 2
        step = d // 2
        return jnp.where(lax.rem(d, 2) == 0, half + step, half - step)

    def send(src, dst, ssem, rsem, **device):
        pltpu.make_async_remote_copy(
            src_ref=src, dst_ref=dst, send_sem=ssem, recv_sem=rsem,
            device_id=device, device_id_type=MESH,
        ).start()

    def drain(ref, sem):
        pltpu.make_async_copy(ref, ref, sem).wait()

    def loop(lower, upper, body):
        def step(i, carry):
            body(i)
            return carry
        lax.fori_loop(lower, upper, step, 0)

    def rows(index, count):
        return pl.ds(pl.multiple_of(index * count, count), count)

    cuts = 4 if units % (4 * LANES) == 0 else 1
    span_in = units // cuts
    loads = []
    for i in range(cuts):
        at = pl.ds(i * span_in, span_in)
        loads.append(pltpu.make_async_copy(hid_hbm.at[:, at], hid.at[:, at], in_sem.at[2 * i]))
        loads.append(pltpu.make_async_copy(down_hbm.at[:, at], down.at[:, at], in_sem.at[2 * i + 1]))
    loads.append(pltpu.make_async_copy(cot_hbm, cot, in_sem.at[2 * cuts]))
    loads.append(pltpu.make_async_copy(up_hbm, up, in_sem.at[2 * cuts + 1]))
    for copy in loads:
        copy.start()
    late = [
        pltpu.make_async_copy(left_hbm, left_buf, left_sem.at[0]),
        pltpu.make_async_copy(right_hbm, right_prev, left_sem.at[1]),
    ]

    barrier = pltpu.get_barrier_semaphore()

    def greet(**device):
        pl.semaphore_signal(barrier, inc=1, device_id=device, device_id_type=MESH)

    loop(1, nz, lambda d: greet(dp=y * nz + z_of(far_first(d))))
    loop(1, n_mp, lambda d: greet(mp=mp_peer(d)))
    loop(1, ny, lambda d: greet(dp=y_of(d) * nz + z))

    def greet_owner(k):
        owner = k * n_mp + mp

        @pl.when(owner != dp)
        def _():
            greet(dp=owner)

    loop(0, owners, greet_owner)

    @pl.when(active)
    def _():
        loop(1, n_dp, lambda d: greet(dp=lax.rem(dp + d, n_dp)))

    acc = jnp.zeros((rank, tok), F32)
    for i in range(cuts):
        loads[2 * i].wait()
        loads[2 * i + 1].wait()
        at = pl.ds(i * span_in, span_in)
        acc = acc + dot1(down[:, at], hid[:, at], NT)
    pbuf[mp, :rank] = acc.astype(BF16)
    loads[-2].wait()
    loads[-1].wait()
    pbuf[mp, rank:] = dot1(up[...], cot[...], NT).astype(BF16)

    common = (n_mp - 1) + (ny - 1) + (nz - 1) + owners
    pl.semaphore_wait(barrier, jnp.where(active, common - 1 + n_dp - 1, common))

    loop(1, n_mp, lambda d: send(pbuf.at[mp], pbuf.at[mp], s_a, r_a, mp=mp_peer(d)))

    @pl.when(active)
    def _():
        for copy in late:
            copy.start()

    drain(pbuf.at[pl.ds(0, n_mp - 1)], r_a)
    acc = pbuf[0].astype(F32)
    for d in range(1, n_mp):
        acc = acc + pbuf[d].astype(F32)
    inner_t, outer_t = acc[:rank].astype(BF16), acc[rank:].astype(BF16)

    def lanes(c):
        return c * tile * LANES, c * tile * LANES + sizes[c] * LANES

    for c in range(chunks):
        lo, hi = lanes(c)
        for at in range(lo, hi, width):
            if at < units:
                piece = dot1(outer_t, hid[:, at:at + width], NN)
            else:
                piece = dot1(inner_t, cot[:, at - units:at - units + width], NN)
            gsend[:, :, at:at + width] = piece.astype(BF16).reshape(ny, rows_y, width)
        span = pl.ds(lo, hi - lo)
        loop(1, ny, lambda d: send(
            gsend.at[y_of(d), :, span], yrecv.at[d - 1, :, span],
            s_y.at[c], r_y.at[c], dp=y_of(d) * nz + z))

    groups = n_mp
    mine = [owner_ref[mp, b] for b in range(nb)]
    zero = jnp.int32(0)

    def scan(i, carry):
        first, second, slot = carry
        g = groups * nb - 1 - i
        value = owner_ref[g // nb, lax.rem(g, nb)]
        hits = [value == k * n_mp + mp for k in range(owners)]
        second = tuple(jnp.where(h, f, s) for h, f, s in zip(hits, first, second))
        first = tuple(jnp.where(h, g, f) for h, f in zip(hits, first))
        slot = tuple(
            v + jnp.where(value == mine[b], jnp.where(g < mp * nb + b, 1, 0), 0)
            for b, v in enumerate(slot))
        return first, second, slot

    first, second, slot = lax.fori_loop(
        0, groups * nb, scan, ((zero,) * owners, (zero,) * owners, (zero,) * nb))
    places = [
        lax.rem(mine[b], n_mp) * (owners * slab) + (mine[b] // n_mp) * slab + slot[b] * parts
        for b in range(nb)]

    scale = ADAPTER_SCALE / (tok * n_dp)
    for c in range(chunks):
        lo, hi = lanes(c)
        drain(yrecv.at[:, :, pl.ds(lo, hi - lo)], r_y.at[c])
        acc = gsend[y, :, lo:hi].astype(F32)
        for d in range(ny - 1):
            acc = acc + yrecv[d, :, lo:hi].astype(F32)
        if c < whole:
            for t in range(tile):
                zstage[c, pl.ds(t, nz, stride=tile), :] = acc[:, t * LANES:(t + 1) * LANES]
            zsend[c] = zstage[c].reshape(nz, tile, LANES).astype(BF16)
            src, dst = zsend.at[c], zrecv.at[c]
        else:
            for t in range(rest):
                rstage[pl.ds(t, nz, stride=8), :] = acc[:, t * LANES:(t + 1) * LANES]
            for i in range(nz):
                rsend[i] = rstage[8 * i:8 * i + rest, :]
            src, dst = rsend, rrecv

        def scatter(i):
            d = far_first(i)
            send(src.at[z_of(d)], dst.at[d - 1], s_z.at[c], r_z.at[c], dp=y * nz + z_of(d))

        loop(1, nz, scatter)
    for c in range(chunks):
        if c < whole:
            drain(zrecv.at[c], r_z.at[c])
            acc = zstage[c, rows(z, tile), :] + jnp.sum(zrecv[c].astype(F32), axis=0)
            grow[c * tile:(c + 1) * tile] = acc * scale
        else:
            drain(rrecv, r_z.at[c])
            acc = rsend[z] + jnp.sum(rrecv[...], axis=0)
            grow[c * tile:c * tile + rest] = acc * scale
            if grow.shape[0] > c * tile + rest:
                grow[c * tile + rest:] = jnp.zeros((grow.shape[0] - c * tile - rest, LANES), F32)

    mpbuf[mp] = grow[...]
    loop(1, n_mp, lambda d: send(grow, mpbuf.at[mp], s_d1, r_d1, mp=mp_peer(d)))
    drain(mpbuf.at[pl.ds(0, n_mp - 1)], r_d1)
    for k in range(owners):
        for s, g in enumerate((first[k], second[k])):
            dsend[k, s * parts:(s + 1) * parts] = mpbuf[
                g // nb, pl.ds(lax.rem(g, nb) * parts, parts), :]

    def to_owner(k):
        owner = k * n_mp + mp

        @pl.when(owner != dp)
        def _():
            send(dsend.at[k], drecv.at[rows(dp, slab)], s_d2, r_d2, dp=owner)

    loop(0, owners, to_owner)

    @pl.when(active)
    def _():
        drecv[rows(dp, slab), :] = dsend[my_k]
        for copy in late:
            copy.wait()
        drain(drecv.at[pl.ds(0, (n_dp - 1) * slab)], r_d2)
        blocks = [
            jnp.concatenate(
                [drecv[pl.ds(s * parts + p, n_dp, stride=slab), :] for p in range(parts)], axis=1)
            for s in range(cap)]
        results = precondition(
            blocks, [left_buf[s] for s in range(cap)], [right_prev[s] for s in range(cap)])
        for s in range(cap):
            for p in range(parts):
                fsend[pl.ds(s * parts + p, n_dp, stride=slab), :] = results[s][
                    :, p * LANES:(p + 1) * LANES]

        def to_home(i):
            d = i // ny + 1
            home = y_of(lax.rem(i, ny)) * nz + z_of(far_first(d))
            send(fsend.at[rows(home, slab)], frecv.at[rows(my_k, slab)], s_f1, r_f1, dp=home)

        loop(0, (nz - 1) * ny, to_home)

        def to_column(d):
            home = y_of(d) * nz + z
            send(fsend.at[rows(home, slab)], frecv.at[rows(my_k, slab)], s_f1, r_f1, dp=home)

        loop(1, ny, to_column)
        frecv[rows(my_k, slab), :] = fsend[rows(dp, slab), :]
        drain(frecv.at[pl.ds(0, (owners - 1) * slab)], r_f1)

    @pl.when(jnp.logical_not(active))
    def _():
        drain(frecv, r_f1)

    fb[...] = frecv[...].astype(BF16)
    fmp[mp] = fb[...]
    loop(1, n_mp, lambda d: send(fb, fmp.at[mp], s_f2, r_f2, mp=mp_peer(d)))
    drain(fmp.at[pl.ds(0, n_mp - 1)], r_f2)
    fmpf[...] = fmp[...].astype(F32).reshape(fmpf.shape)
    for b in range(nb):
        hrow[b * parts:(b + 1) * parts] = fmpf[pl.ds(places[b], parts), :]
    for c in range(chunks):
        if c < whole:
            fin[c, z] = hrow[c * tile:(c + 1) * tile].astype(BF16)
            buf = fin.at[c]
        else:
            finr[z] = hrow[c * tile:c * tile + rest]
            buf = finr

        def spread(i):
            d = far_first(i)
            send(buf.at[z], buf.at[z], s_fz.at[c], r_fz.at[c], dp=y * nz + z_of(d))

        loop(1, nz, spread)

    def spans(c):
        lo, hi = lanes(c)
        found = []
        if lo < units:
            found.append((out_a, lo, lo, min(hi, units) - lo))
        if hi > units:
            start = max(lo, units)
            found.append((out_b, start, start - units, hi - start))
        return found

    mine_rows = rows(y, rows_y)
    for c in range(chunks):
        if c < whole:
            drain(fin.at[c, pl.ds(0, nz - 1)], r_fz.at[c])
            finf[...] = fin[c].astype(F32).reshape(finf.shape)
            for t in range(tile):
                at = (c * tile + t) * LANES
                ystage[:, at:at + LANES] = finf[pl.ds(t, nz, stride=tile), :].astype(BF16)
        else:
            drain(finr.at[pl.ds(0, nz - 1)], r_fz.at[c])
            for i in range(nz):
                finrf[8 * i:8 * i + rest, :] = finr[i]
            for t in range(rest):
                at = (c * tile + t) * LANES
                ystage[:, at:at + LANES] = finrf[pl.ds(t, nz, stride=8), :].astype(BF16)
        for j, (out, src, dst, count) in enumerate(spans(c)):
            loop(1, ny, lambda d: send(
                ystage.at[:, pl.ds(src, count)], out.at[mine_rows, pl.ds(dst, count)],
                s_fy.at[2 * c + j], r_fy.at[2 * c + j], dp=y_of(d) * nz + z))
            pltpu.make_async_copy(
                ystage.at[:, pl.ds(src, count)], out.at[mine_rows, pl.ds(dst, count)],
                own_sem.at[2 * c + j]).start()
    for c in range(chunks):
        for j, (out, src, dst, count) in enumerate(spans(c)):
            arrived = out.at[pl.ds(0, rank - rows_y), pl.ds(dst, count)]
            drain(arrived, r_fy.at[2 * c + j])
            drain(arrived, s_fy.at[2 * c + j])
            pltpu.make_async_copy(
                ystage.at[:, pl.ds(src, count)], out.at[mine_rows, pl.ds(dst, count)],
                own_sem.at[2 * c + j]).wait()

    drain(pbuf.at[pl.ds(0, n_mp - 1)], s_a)
    for c in range(chunks):
        lo, hi = lanes(c)
        drain(yrecv.at[:, :, pl.ds(lo, hi - lo)], s_y.at[c])
        if c < whole:
            drain(zrecv.at[c], s_z.at[c])
            drain(fin.at[c, pl.ds(0, nz - 1)], s_fz.at[c])
        else:
            drain(rrecv, s_z.at[c])
            drain(finr.at[pl.ds(0, nz - 1)], s_fz.at[c])
    drain(mpbuf.at[pl.ds(0, n_mp - 1)], s_d1)
    drain(fmp.at[pl.ds(0, n_mp - 1)], s_f2)

    @pl.when(active)
    def _():
        drain(dsend.at[pl.ds(0, owners - 1)], s_d2)
        drain(fsend.at[pl.ds(0, (n_dp - 1) * slab)], s_f1)

    @pl.when(jnp.logical_not(active))
    def _():
        drain(dsend, s_d2)


def placing(first_in, second_in, first_out, second_out):
    first_out[...] = first_in[...]
    second_out[...] = second_in[...]


def shards(
    hidden, cotangent, adapter_down, adapter_up, owner_per_block, left_statistics, right_statistics
):
    n_dp, n_mp = lax.axis_size("dp"), lax.axis_size("mp")
    nz = Z_EXTENT
    ny = n_dp // nz
    tok, units = hidden.shape
    features = cotangent.shape[1]
    rank = adapter_down.shape[1]
    nb = owner_per_block.shape[1]
    cap, width = left_statistics.shape[:2]
    parts = width // LANES
    owners = n_dp // n_mp
    tile = BLOCKS_PER_CHUNK * parts
    whole = nb // BLOCKS_PER_CHUNK
    chunks = whole + 1
    rest = (nb - whole * BLOCKS_PER_CHUNK) * parts
    slab = cap * parts
    keep = -(-nb * parts // 8) * 8
    rows_y = rank // ny

    any_space = pl.BlockSpec(memory_space=pl.ANY)
    dma = pltpu.SemaphoreType.DMA
    vmem = pltpu.VMEM
    cfg = (n_dp, n_mp, ny, nz, rank, width, nb, cap)
    shapes = (
        jax.ShapeDtypeStruct((rank, units), BF16),
        jax.ShapeDtypeStruct((rank, features), BF16),
    )
    update_a, update_b = pl.pallas_call(
        functools.partial(kernel, cfg),
        out_shape=shapes,
        in_specs=[pl.BlockSpec(memory_space=pltpu.SMEM)] + [any_space] * 6,
        out_specs=(any_space, any_space),
        scratch_shapes=[
            vmem((tok, units), BF16),
            vmem((tok, features), BF16),
            vmem((rank, units), BF16),
            vmem((rank, features), BF16),
            vmem((cap, rank, rank), F32),
            vmem((cap, width, width), F32),
            vmem((n_mp, 2 * rank, tok), BF16),
            vmem((ny, rows_y, nb * width), BF16),
            vmem((ny - 1, rows_y, nb * width), BF16),
            vmem((whole, nz * tile, LANES), F32),
            vmem((whole, nz, tile, LANES), BF16),
            vmem((whole, nz - 1, tile, LANES), BF16),
            vmem((nz * 8, LANES), F32),
            vmem((nz, rest, LANES), F32),
            vmem((nz - 1, rest, LANES), F32),
            vmem((keep, LANES), F32),
            vmem((n_mp, keep, LANES), F32),
            vmem((owners, slab, LANES), F32),
            vmem((n_dp * slab, LANES), F32),
            vmem((n_dp * slab, LANES), F32),
            vmem((owners * slab, LANES), F32),
            vmem((owners * slab, LANES), BF16),
            vmem((n_mp, owners * slab, LANES), BF16),
            vmem((n_mp * owners * slab, LANES), F32),
            vmem((keep, LANES), F32),
            vmem((whole, nz, tile, LANES), BF16),
            vmem((nz, rest, LANES), F32),
            vmem((nz * tile, LANES), F32),
            vmem((nz * 8, LANES), F32),
            vmem((rows_y, nb * width), BF16),
            dma((10,)), dma((2,)), dma, dma,
            dma((chunks,)), dma((chunks,)), dma((chunks,)), dma((chunks,)),
            dma, dma, dma, dma, dma, dma, dma, dma,
            dma((chunks,)), dma((chunks,)),
            dma((2 * chunks,)), dma((2 * chunks,)), dma((2 * chunks,)),
        ],
        compiler_params=pltpu.CompilerParams(
            collective_id=0, has_side_effects=True, vmem_limit_bytes=58 * 1024 * 1024
        ),
    )(
        owner_per_block, hidden, cotangent, adapter_down.T, adapter_up,
        left_statistics, right_statistics,
    )
    update_a, update_b = pl.pallas_call(
        placing,
        out_shape=shapes,
        in_specs=[pl.BlockSpec(memory_space=vmem)] * 2,
        out_specs=(pl.BlockSpec(memory_space=vmem), pl.BlockSpec(memory_space=vmem)),
        compiler_params=pltpu.CompilerParams(vmem_limit_bytes=58 * 1024 * 1024),
    )(update_a, update_b)
    return update_a.T, update_b


def solution(mesh):
    return jax.shard_map(
        shards,
        mesh=mesh,
        in_specs=(
            P("dp", "mp"),
            P("dp", "mp"),
            P("mp", None),
            P(None, "mp"),
            P(),
            P("dp", None, None),
            P("dp", None, None),
        ),
        out_specs=(P("mp", None), P(None, "mp")),
        check_vma=False,
    )
```

time: 109 us -> 87 us (0.80)
  Pallas kernels: 97.6 us -> 86.2 us
  local copies, waits for them, and re-layouts: 9.39 us -> 0 us
    pallas_call x1 -> x2, Pallas kernels: 97.6 us -> 86.2 us  [the longest x1 84.3 us: shards(): pl.pallas_call(functools.partial(kernel, cfg), out_shape=shapes, in_specs...]
    unnamed x12 -> x0, local copies, waits for them, and re-layouts: 7.56 us -> none
where the time goes in v2:
time: 87 us; the launch traced here: 86.8 us
  Pallas kernels  86.2 us (99%)
    pallas_call x1, Pallas kernels, shards(): pl.pallas_call(functools.partial(kernel, cfg), out_shape=shapes, in_specs...  84.3 us
    pallas_call x1, Pallas kernels, shards(): pl.pallas_call(placing, out_shape=shapes, in_specs=[pl.BlockSpec(memory_s...  1.88 us

profile of v2, /device:TPU:1, one launch (start us, length us, event | category | flops | bytes accessed | tf_op | source)
XLA Modules:
  0.0 86.8 jit_solution(14639942159230780854)
XLA Ops:
  0.6 84.3 %shard_map.86 = (bf16[64,3584]{1,0:T(8,128)(2,1)}, bf16[64,1024]{1,0:T(8,128)(2,1)}) custom-call(s32[8,9]{1,0:T(8,128)} %owner_ref.1, bf16[128,3584]{1,0:T(8,128)(2,1)} %hid_hbm.1, bf16[128,1024]{1,0:T(8,128)(2,1)} %cot_hbm.1, bf16[64,3584]{1,0:T(8,128)(2,1)} %bitcast.2, bf16[64,1024]{1,0:T(8,128)(2,1)} %up_hbm.1, f32[2,512,512]{2,1,0:T(8,128)} %left_hbm.1, ...), custom_call_target="tpu_custom_call" | custom-call | tf_op jit(solution)/shard_map/pallas_call | solution.py:447
  84.9 1.9 %shard_map.87 = (bf16[64,3584]{1,0:T(8,128)(2,1)}, bf16[64,1024]{1,0:T(8,128)(2,1)}) custom-call(bf16[64,3584]{1,0:T(8,128)(2,1)} %get-tuple-element.6.first_in, bf16[64,1024]{1,0:T(8,128)(2,1)} %get-tuple-element.7.second_in), custom_call_target="tpu_custom_call" | custom-call | tf_op jit(solution)/shard_map/pallas_call | solution.py:496

commit v3 on v2

--- a/solution.py
+++ b/solution.py
@@ -92,6 +92,8 @@
     sizes = [tile] * whole + [rest]
     tok, units = hid.shape
     slab = cap * parts
+    half = nz // 2
+    pair = 2 * slab
     rows_y = rank // ny
     blocks_a = units // width
 
@@ -111,7 +113,6 @@
         return lax.rem(z + d, nz)
 
     def far_first(d):
-        half = nz // 2
         step = d // 2
         return jnp.where(lax.rem(d, 2) == 0, half + step, half - step)
 
@@ -158,19 +159,6 @@
     loop(1, n_mp, lambda d: greet(mp=mp_peer(d)))
     loop(1, ny, lambda d: greet(dp=y_of(d) * nz + z))
 
-    def greet_owner(k):
-        owner = k * n_mp + mp
-
-        @pl.when(owner != dp)
-        def _():
-            greet(dp=owner)
-
-    loop(0, owners, greet_owner)
-
-    @pl.when(active)
-    def _():
-        loop(1, n_dp, lambda d: greet(dp=lax.rem(dp + d, n_dp)))
-
     acc = jnp.zeros((rank, tok), F32)
     for i in range(cuts):
         loads[2 * i].wait()
@@ -182,8 +170,7 @@
     loads[-1].wait()
     pbuf[mp, rank:] = dot1(up[...], cot[...], NT).astype(BF16)
 
-    common = (n_mp - 1) + (ny - 1) + (nz - 1) + owners
-    pl.semaphore_wait(barrier, jnp.where(active, common - 1 + n_dp - 1, common))
+    pl.semaphore_wait(barrier, (n_mp - 1) + (ny - 1) + (nz - 1))
 
     loop(1, n_mp, lambda d: send(pbuf.at[mp], pbuf.at[mp], s_a, r_a, mp=mp_peer(d)))
 
@@ -233,7 +220,7 @@
     first, second, slot = lax.fori_loop(
         0, groups * nb, scan, ((zero,) * owners, (zero,) * owners, (zero,) * nb))
     places = [
-        lax.rem(mine[b], n_mp) * (owners * slab) + (mine[b] // n_mp) * slab + slot[b] * parts
+        lax.rem(mine[b], n_mp) * (owners * pair) + (mine[b] // n_mp) * pair + slot[b] * parts
         for b in range(nb)]
 
     scale = ADAPTER_SCALE / (tok * n_dp)
@@ -303,23 +290,26 @@
             blocks, [left_buf[s] for s in range(cap)], [right_prev[s] for s in range(cap)])
         for s in range(cap):
             for p in range(parts):
-                fsend[pl.ds(s * parts + p, n_dp, stride=slab), :] = results[s][
-                    :, p * LANES:(p + 1) * LANES]
+                for q in range(2 * ny):
+                    fsend[pl.ds((q // 2) * half * pair + (q % 2) * slab + s * parts + p, half, stride=pair), :] = (
+                        results[s][q * half:(q + 1) * half, p * LANES:(p + 1) * LANES])
+
+        def home_rows(yy, zz):
+            return rows(yy * half + lax.rem(zz, half), pair)
 
         def to_home(i):
-            d = i // ny + 1
-            home = y_of(lax.rem(i, ny)) * nz + z_of(far_first(d))
-            send(fsend.at[rows(home, slab)], frecv.at[rows(my_k, slab)], s_f1, r_f1, dp=home)
+            yy, zz = y_of(lax.rem(i, ny)), z_of(far_first(i // ny + 1))
+            send(fsend.at[home_rows(yy, zz)], frecv.at[rows(my_k, pair)], s_f1, r_f1, dp=yy * nz + zz)
 
         loop(0, (nz - 1) * ny, to_home)
 
         def to_column(d):
-            home = y_of(d) * nz + z
-            send(fsend.at[rows(home, slab)], frecv.at[rows(my_k, slab)], s_f1, r_f1, dp=home)
+            send(fsend.at[home_rows(y_of(d), z)], frecv.at[rows(my_k, pair)], s_f1, r_f1,
+                 dp=y_of(d) * nz + z)
 
         loop(1, ny, to_column)
-        frecv[rows(my_k, slab), :] = fsend[rows(dp, slab), :]
-        drain(frecv.at[pl.ds(0, (owners - 1) * slab)], r_f1)
+        frecv[rows(my_k, pair), :] = fsend[home_rows(y, z), :]
+        drain(frecv.at[pl.ds(0, (owners - 1) * pair)], r_f1)
 
     @pl.when(jnp.logical_not(active))
     def _():
@@ -330,21 +320,24 @@
     loop(1, n_mp, lambda d: send(fb, fmp.at[mp], s_f2, r_f2, mp=mp_peer(d)))
     drain(fmp.at[pl.ds(0, n_mp - 1)], r_f2)
     fmpf[...] = fmp[...].astype(F32).reshape(fmpf.shape)
-    for b in range(nb):
-        hrow[b * parts:(b + 1) * parts] = fmpf[pl.ds(places[b], parts), :]
-    for c in range(chunks):
-        if c < whole:
-            fin[c, z] = hrow[c * tile:(c + 1) * tile].astype(BF16)
-            buf = fin.at[c]
-        else:
-            finr[z] = hrow[c * tile:c * tile + rest]
-            buf = finr
+    for h in range(2):
+        for b in range(nb):
+            hrow[h, b * parts:(b + 1) * parts] = fmpf[pl.ds(places[b] + h * slab, parts), :]
+    kind = lax.rem(z, half)
+    for c in range(chunks):
+        for h in range(2):
+            if c < whole:
+                fin[c, kind, h] = hrow[h, c * tile:(c + 1) * tile].astype(BF16)
+            else:
+                finr[kind, h] = hrow[h, c * tile:c * tile + rest]
+        buf = fin.at[c] if c < whole else finr
 
         def spread(i):
-            d = far_first(i)
-            send(buf.at[z], buf.at[z], s_fz.at[c], r_fz.at[c], dp=y * nz + z_of(d))
-
-        loop(1, nz, spread)
+            up_to = half // 2
+            d = jnp.where(i < up_to, up_to - i, nz - (half - 1 - i))
+            send(buf.at[kind], buf.at[kind], s_fz.at[c], r_fz.at[c], dp=y * nz + z_of(d))
+
+        loop(0, half - 1, spread)
 
     def spans(c):
         lo, hi = lanes(c)
@@ -359,15 +352,19 @@
     mine_rows = rows(y, rows_y)
     for c in range(chunks):
         if c < whole:
-            drain(fin.at[c, pl.ds(0, nz - 1)], r_fz.at[c])
+            drain(fin.at[c, pl.ds(0, half - 1)], r_fz.at[c])
             finf[...] = fin[c].astype(F32).reshape(finf.shape)
             for t in range(tile):
                 at = (c * tile + t) * LANES
-                ystage[:, at:at + LANES] = finf[pl.ds(t, nz, stride=tile), :].astype(BF16)
+                ystage[:, at:at + LANES] = jnp.concatenate(
+                    [finf[pl.ds(h * tile + t, half, stride=2 * tile), :] for h in range(2)],
+                    axis=0).astype(BF16)
         else:
-            drain(finr.at[pl.ds(0, nz - 1)], r_fz.at[c])
-            for i in range(nz):
-                finrf[8 * i:8 * i + rest, :] = finr[i]
+            drain(finr.at[pl.ds(0, half - 1)], r_fz.at[c])
+            for i in range(half):
+                for h in range(2):
+                    at = 8 * (h * half + i)
+                    finrf[at:at + rest, :] = finr[i, h]
             for t in range(rest):
                 at = (c * tile + t) * LANES
                 ystage[:, at:at + LANES] = finrf[pl.ds(t, nz, stride=8), :].astype(BF16)
@@ -393,17 +390,17 @@
         drain(yrecv.at[:, :, pl.ds(lo, hi - lo)], s_y.at[c])
         if c < whole:
             drain(zrecv.at[c], s_z.at[c])
-            drain(fin.at[c, pl.ds(0, nz - 1)], s_fz.at[c])
+            drain(fin.at[c, pl.ds(0, half - 1)], s_fz.at[c])
         else:
             drain(rrecv, s_z.at[c])
-            drain(finr.at[pl.ds(0, nz - 1)], s_fz.at[c])
+            drain(finr.at[pl.ds(0, half - 1)], s_fz.at[c])
     drain(mpbuf.at[pl.ds(0, n_mp - 1)], s_d1)
     drain(fmp.at[pl.ds(0, n_mp - 1)], s_f2)
 
     @pl.when(active)
     def _():
         drain(dsend.at[pl.ds(0, owners - 1)], s_d2)
-        drain(fsend.at[pl.ds(0, (n_dp - 1) * slab)], s_f1)
+        drain(fmpf.at[pl.ds(0, (n_dp - 1) * pair)], s_f1)
 
     @pl.when(jnp.logical_not(active))
     def _():
@@ -470,13 +467,13 @@
             vmem((owners, slab, LANES), F32),
             vmem((n_dp * slab, LANES), F32),
             vmem((n_dp * slab, LANES), F32),
-            vmem((owners * slab, LANES), F32),
-            vmem((owners * slab, LANES), BF16),
-            vmem((n_mp, owners * slab, LANES), BF16),
-            vmem((n_mp * owners * slab, LANES), F32),
-            vmem((keep, LANES), F32),
-            vmem((whole, nz, tile, LANES), BF16),
-            vmem((nz, rest, LANES), F32),
+            vmem((2 * owners * slab, LANES), F32),
+            vmem((2 * owners * slab, LANES), BF16),
+            vmem((n_mp, 2 * owners * slab, LANES), BF16),
+            vmem((2 * n_mp * owners * slab, LANES), F32),
+            vmem((2, keep, LANES), F32),
+            vmem((whole, nz // 2, 2, tile, LANES), BF16),
+            vmem((nz // 2, 2, rest, LANES), F32),
             vmem((nz * tile, LANES), F32),
             vmem((nz * 8, LANES), F32),
             vmem((rows_y, nb * width), BF16),

time: 87 us -> 85.3 us (0.980)
  Pallas kernels: 86.2 us -> 84.4 us
    pallas_call x1, Pallas kernels: 84.3 us -> 82.6 us  [shards(): pl.pallas_call(functools.partial(kernel, cfg), out_shape=shapes, in_specs...]
where the time goes in v3:
time: 85.3 us; the launch traced here: 85.1 us
  Pallas kernels  84.4 us (99%)
    pallas_call x1, Pallas kernels, shards(): pl.pallas_call(functools.partial(kernel, cfg), out_shape=shapes, in_specs...  82.6 us
    pallas_call x1, Pallas kernels, shards(): pl.pallas_call(placing, out_shape=shapes, in_specs=[pl.BlockSpec(memory_s...  1.88 us

profile of v3, /device:TPU:1, one launch (start us, length us, event | category | flops | bytes accessed | tf_op | source)
XLA Modules:
  0.0 85.1 jit_solution(14477520575465268546)
XLA Ops:
  0.6 82.6 %shard_map.86 = (bf16[64,3584]{1,0:T(8,128)(2,1)}, bf16[64,1024]{1,0:T(8,128)(2,1)}) custom-call(s32[8,9]{1,0:T(8,128)} %owner_ref.1, bf16[128,3584]{1,0:T(8,128)(2,1)} %hid_hbm.1, bf16[128,1024]{1,0:T(8,128)(2,1)} %cot_hbm.1, bf16[64,3584]{1,0:T(8,128)(2,1)} %bitcast.2, bf16[64,1024]{1,0:T(8,128)(2,1)} %up_hbm.1, f32[2,512,512]{2,1,0:T(8,128)} %left_hbm.1, ...), custom_call_target="tpu_custom_call" | custom-call | tf_op jit(solution)/shard_map/pallas_call | solution.py:444
  83.2 1.9 %shard_map.87 = (bf16[64,3584]{1,0:T(8,128)(2,1)}, bf16[64,1024]{1,0:T(8,128)(2,1)}) custom-call(bf16[64,3584]{1,0:T(8,128)(2,1)} %get-tuple-element.6.first_in, bf16[64,1024]{1,0:T(8,128)(2,1)} %get-tuple-element.7.second_in), custom_call_target="tpu_custom_call" | custom-call | tf_op jit(solution)/shard_map/pallas_call | solution.py:493

commit v4 on v3

--- a/solution.py
+++ b/solution.py
@@ -77,7 +77,7 @@
     owner_ref, hid_hbm, cot_hbm, down_hbm, up_hbm, left_hbm, right_hbm,
     out_a, out_b,
     hid, cot, down, up, right_prev, left_buf, pbuf, gsend, yrecv, zstage, zsend, zrecv,
-    rstage, rsend, rrecv, grow, mpbuf, dsend, drecv, fsend, frecv, fb, fmp, fmpf, hrow,
+    rstage, rsend, rrecv, grow, growb, mpbuf, mpf, dsend, drecv, fsend, frecv, fb, fmp, fmpf, hrow,
     fin, finr, finf, finrf, ystage,
     in_sem, left_sem, s_a, r_a, s_y, r_y, s_z, r_z, s_d1, r_d1, s_d2, r_d2,
     s_f1, r_f1, s_f2, r_f2, s_fz, r_fz, s_fy, r_fy, own_sem,
@@ -89,6 +89,7 @@
     whole = nb // BLOCKS_PER_CHUNK
     chunks = whole + 1
     rest = (nb - whole * BLOCKS_PER_CHUNK) * parts
+    keep = -(-nb * parts // 8) * 8
     sizes = [tile] * whole + [rest]
     tok, units = hid.shape
     slab = cap * parts
@@ -102,6 +103,7 @@
     y, z = dp // nz, lax.rem(dp, nz)
     active = lax.rem(dp, n_mp) == mp
     my_k = dp // n_mp
+    kind = lax.rem(z, half)
 
     def mp_peer(d):
         return lax.rem(mp + d, n_mp)
@@ -115,6 +117,10 @@
     def far_first(d):
         step = d // 2
         return jnp.where(lax.rem(d, 2) == 0, half + step, half - step)
+
+    def near(i):
+        up_to = half // 2
+        return jnp.where(i < up_to, up_to - i, nz - (half - 1 - i))
 
     def send(src, dst, ssem, rsem, **device):
         pltpu.make_async_remote_copy(
@@ -232,59 +238,75 @@
             acc = acc + yrecv[d, :, lo:hi].astype(F32)
         if c < whole:
             for t in range(tile):
-                zstage[c, pl.ds(t, nz, stride=tile), :] = acc[:, t * LANES:(t + 1) * LANES]
-            zsend[c] = zstage[c].reshape(nz, tile, LANES).astype(BF16)
+                for h in range(2):
+                    zstage[c, pl.ds(h * tile + t, half, stride=2 * tile), :] = (
+                        acc[h * half:(h + 1) * half, t * LANES:(t + 1) * LANES])
+            zsend[c] = zstage[c].reshape(half, 2, tile, LANES).astype(BF16)
             src, dst = zsend.at[c], zrecv.at[c]
         else:
             for t in range(rest):
                 rstage[pl.ds(t, nz, stride=8), :] = acc[:, t * LANES:(t + 1) * LANES]
             for i in range(nz):
-                rsend[i] = rstage[8 * i:8 * i + rest, :]
+                rsend[i % half, i // half] = rstage[8 * i:8 * i + rest, :]
             src, dst = rsend, rrecv
 
         def scatter(i):
-            d = far_first(i)
-            send(src.at[z_of(d)], dst.at[d - 1], s_z.at[c], r_z.at[c], dp=y * nz + z_of(d))
-
-        loop(1, nz, scatter)
+            home = z_of(near(i))
+            send(src.at[lax.rem(home, half)], dst.at[i], s_z.at[c], r_z.at[c], dp=y * nz + home)
+
+        loop(0, half - 1, scatter)
     for c in range(chunks):
         if c < whole:
             drain(zrecv.at[c], r_z.at[c])
-            acc = zstage[c, rows(z, tile), :] + jnp.sum(zrecv[c].astype(F32), axis=0)
-            grow[c * tile:(c + 1) * tile] = acc * scale
+            others = jnp.sum(zrecv[c].astype(F32), axis=0)
+            for h in range(2):
+                acc = zstage[c, rows(2 * kind + h, tile), :] + others[h]
+                grow[h * keep + c * tile:h * keep + (c + 1) * tile] = acc * scale
         else:
             drain(rrecv, r_z.at[c])
-            acc = rsend[z] + jnp.sum(rrecv[...], axis=0)
-            grow[c * tile:c * tile + rest] = acc * scale
-            if grow.shape[0] > c * tile + rest:
-                grow[c * tile + rest:] = jnp.zeros((grow.shape[0] - c * tile - rest, LANES), F32)
-
-    mpbuf[mp] = grow[...]
-    loop(1, n_mp, lambda d: send(grow, mpbuf.at[mp], s_d1, r_d1, mp=mp_peer(d)))
+            acc = (rsend[kind] + jnp.sum(rrecv[...], axis=0)) * scale
+            for h in range(2):
+                grow[h * keep + c * tile:h * keep + c * tile + rest] = acc[h]
+                used = c * tile + rest
+                if keep > used:
+                    grow[h * keep + used:(h + 1) * keep] = jnp.zeros((keep - used, LANES), F32)
+
+    growb[...] = grow[...].astype(BF16)
+    mpbuf[mp] = growb[...]
+    loop(1, n_mp, lambda d: send(growb, mpbuf.at[mp], s_d1, r_d1, mp=mp_peer(d)))
     drain(mpbuf.at[pl.ds(0, n_mp - 1)], r_d1)
+    mpf[...] = mpbuf[...].astype(F32)
     for k in range(owners):
         for s, g in enumerate((first[k], second[k])):
-            dsend[k, s * parts:(s + 1) * parts] = mpbuf[
-                g // nb, pl.ds(lax.rem(g, nb) * parts, parts), :]
+            for h in range(2):
+                dsend[k, h * slab + s * parts:h * slab + (s + 1) * parts] = mpf[
+                    g // nb, pl.ds(h * keep + lax.rem(g, nb) * parts, parts), :]
 
     def to_owner(k):
         owner = k * n_mp + mp
 
         @pl.when(owner != dp)
         def _():
-            send(dsend.at[k], drecv.at[rows(dp, slab)], s_d2, r_d2, dp=owner)
+            send(dsend.at[k], drecv.at[rows(dp, pair)], s_d2, r_d2, dp=owner)
 
     loop(0, owners, to_owner)
 
     @pl.when(active)
     def _():
-        drecv[rows(dp, slab), :] = dsend[my_k]
+        drecv[rows(dp, pair), :] = dsend[my_k]
         for copy in late:
             copy.wait()
-        drain(drecv.at[pl.ds(0, (n_dp - 1) * slab)], r_d2)
+        drain(drecv.at[pl.ds(0, (n_dp - 1) * pair)], r_d2)
+
+        def part_of(s, p, q):
+            at = (q // 2) * nz * pair + (q % 2) * slab + s * parts + p
+            return (drecv[pl.ds(at, half, stride=pair), :]
+                    + drecv[pl.ds(at + half * pair, half, stride=pair), :])
+
         blocks = [
             jnp.concatenate(
-                [drecv[pl.ds(s * parts + p, n_dp, stride=slab), :] for p in range(parts)], axis=1)
+                [jnp.concatenate([part_of(s, p, q) for q in range(2 * ny)], axis=0)
+                 for p in range(parts)], axis=1)
             for s in range(cap)]
         results = precondition(
             blocks, [left_buf[s] for s in range(cap)], [right_prev[s] for s in range(cap)])
@@ -323,7 +345,6 @@
     for h in range(2):
         for b in range(nb):
             hrow[h, b * parts:(b + 1) * parts] = fmpf[pl.ds(places[b] + h * slab, parts), :]
-    kind = lax.rem(z, half)
     for c in range(chunks):
         for h in range(2):
             if c < whole:
@@ -333,9 +354,7 @@
         buf = fin.at[c] if c < whole else finr
 
         def spread(i):
-            up_to = half // 2
-            d = jnp.where(i < up_to, up_to - i, nz - (half - 1 - i))
-            send(buf.at[kind], buf.at[kind], s_fz.at[c], r_fz.at[c], dp=y * nz + z_of(d))
+            send(buf.at[kind], buf.at[kind], s_fz.at[c], r_fz.at[c], dp=y * nz + z_of(near(i)))
 
         loop(0, half - 1, spread)
 
@@ -457,15 +476,17 @@
             vmem((ny, rows_y, nb * width), BF16),
             vmem((ny - 1, rows_y, nb * width), BF16),
             vmem((whole, nz * tile, LANES), F32),
-            vmem((whole, nz, tile, LANES), BF16),
-            vmem((whole, nz - 1, tile, LANES), BF16),
+            vmem((whole, nz // 2, 2, tile, LANES), BF16),
+            vmem((whole, nz // 2 - 1, 2, tile, LANES), BF16),
             vmem((nz * 8, LANES), F32),
-            vmem((nz, rest, LANES), F32),
-            vmem((nz - 1, rest, LANES), F32),
-            vmem((keep, LANES), F32),
-            vmem((n_mp, keep, LANES), F32),
-            vmem((owners, slab, LANES), F32),
-            vmem((n_dp * slab, LANES), F32),
+            vmem((nz // 2, 2, rest, LANES), F32),
+            vmem((nz // 2 - 1, 2, rest, LANES), F32),
+            vmem((2 * keep, LANES), F32),
+            vmem((2 * keep, LANES), BF16),
+            vmem((n_mp, 2 * keep, LANES), BF16),
+            vmem((n_mp, 2 * keep, LANES), F32),
+            vmem((owners, 2 * slab, LANES), F32),
+            vmem((2 * n_dp * slab, LANES), F32),
             vmem((n_dp * slab, LANES), F32),
             vmem((2 * owners * slab, LANES), F32),
             vmem((2 * owners * slab, LANES), BF16),

time: 85.3 us -> 81.8 us (0.959)
  Pallas kernels: 84.4 us -> 81 us
    pallas_call x1, Pallas kernels: 82.6 us -> 79.1 us  [shards(): pl.pallas_call(functools.partial(kernel, cfg), out_shape=shapes, in_specs...]
where the time goes in v4:
time: 81.8 us; the launch traced here: 81.6 us
  Pallas kernels  81 us (99%)
    pallas_call x1, Pallas kernels, shards(): pl.pallas_call(functools.partial(kernel, cfg), out_shape=shapes, in_specs...  79.1 us
    pallas_call x1, Pallas kernels, shards(): pl.pallas_call(placing, out_shape=shapes, in_specs=[pl.BlockSpec(memory_s...  1.88 us

profile of v4, /device:TPU:1, one launch (start us, length us, event | category | flops | bytes accessed | tf_op | source)
XLA Modules:
  0.0 81.6 jit_solution(2592269693693263302)
XLA Ops:
  0.6 79.1 %shard_map.86 = (bf16[64,3584]{1,0:T(8,128)(2,1)}, bf16[64,1024]{1,0:T(8,128)(2,1)}) custom-call(s32[8,9]{1,0:T(8,128)} %owner_ref.1, bf16[128,3584]{1,0:T(8,128)(2,1)} %hid_hbm.1, bf16[128,1024]{1,0:T(8,128)(2,1)} %cot_hbm.1, bf16[64,3584]{1,0:T(8,128)(2,1)} %bitcast.2, bf16[64,1024]{1,0:T(8,128)(2,1)} %up_hbm.1, f32[2,512,512]{2,1,0:T(8,128)} %left_hbm.1, ...), custom_call_target="tpu_custom_call" | custom-call | tf_op jit(solution)/shard_map/pallas_call | solution.py:463
  79.8 1.9 %shard_map.87 = (bf16[64,3584]{1,0:T(8,128)(2,1)}, bf16[64,1024]{1,0:T(8,128)(2,1)}) custom-call(bf16[64,3584]{1,0:T(8,128)(2,1)} %get-tuple-element.6.first_in, bf16[64,1024]{1,0:T(8,128)(2,1)} %get-tuple-element.7.second_in), custom_call_target="tpu_custom_call" | custom-call | tf_op jit(solution)/shard_map/pallas_call | solution.py:514

commit v5 on v4

--- a/solution.py
+++ b/solution.py
@@ -194,7 +194,7 @@
     def lanes(c):
         return c * tile * LANES, c * tile * LANES + sizes[c] * LANES
 
-    for c in range(chunks):
+    for c in [chunks - 1] + list(range(whole)):
         lo, hi = lanes(c)
         for at in range(lo, hi, width):
             if at < units:
@@ -230,7 +230,7 @@
         for b in range(nb)]
 
     scale = ADAPTER_SCALE / (tok * n_dp)
-    for c in range(chunks):
+    for c in [chunks - 1] + list(range(whole)):
         lo, hi = lanes(c)
         drain(yrecv.at[:, :, pl.ds(lo, hi - lo)], r_y.at[c])
         acc = gsend[y, :, lo:hi].astype(F32)
@@ -255,7 +255,7 @@
             send(src.at[lax.rem(home, half)], dst.at[i], s_z.at[c], r_z.at[c], dp=y * nz + home)
 
         loop(0, half - 1, scatter)
-    for c in range(chunks):
+    for c in [chunks - 1] + list(range(whole)):
         if c < whole:
             drain(zrecv.at[c], r_z.at[c])
             others = jnp.sum(zrecv[c].astype(F32), axis=0)
@@ -426,9 +426,22 @@
         drain(dsend, s_d2)
 
 
-def placing(first_in, second_in, first_out, second_out):
-    first_out[...] = first_in[...]
-    second_out[...] = second_in[...]
+def placing(first_in, second_in, first_out, second_out, first, second, sem_in, sem_out):
+    pieces = []
+    for source, held, target in ((first_in, first, first_out), (second_in, second, second_out)):
+        step = max(16, source.shape[0] // 4)
+        for at in range(0, source.shape[0], step):
+            span = pl.ds(at, min(step, source.shape[0] - at))
+            pieces.append((source.at[span], held.at[span], target.at[span]))
+    inward = [pltpu.make_async_copy(a, b, sem_in.at[i]) for i, (a, b, _) in enumerate(pieces)]
+    outward = [pltpu.make_async_copy(b, c, sem_out.at[i]) for i, (_, b, c) in enumerate(pieces)]
+    for copy in inward:
+        copy.start()
+    for first_half, second_half in zip(inward, outward):
+        first_half.wait()
+        second_half.start()
+    for copy in outward:
+        copy.wait()
 
 
 def shards(
@@ -514,8 +527,11 @@
     update_a, update_b = pl.pallas_call(
         placing,
         out_shape=shapes,
-        in_specs=[pl.BlockSpec(memory_space=vmem)] * 2,
-        out_specs=(pl.BlockSpec(memory_space=vmem), pl.BlockSpec(memory_space=vmem)),
+        in_specs=[any_space] * 2,
+        out_specs=(any_space, any_space),
+        scratch_shapes=[
+            vmem((rank, units), BF16), vmem((rank, features), BF16), dma((8,)), dma((8,)),
+        ],
         compiler_params=pltpu.CompilerParams(vmem_limit_bytes=58 * 1024 * 1024),
     )(update_a, update_b)
     return update_a.T, update_b

time: 81.8 us -> 80.7 us (0.987)
  Pallas kernels: 81 us -> 79.9 us
    pallas_call x1, Pallas kernels: 79.1 us -> 78 us  [shards(): pl.pallas_call(functools.partial(kernel, cfg), out_shape=shapes, in_specs...]
where the time goes in v5:
time: 80.7 us; the launch traced here: 80.5 us
  Pallas kernels  79.9 us (99%)
    pallas_call x1, Pallas kernels, shards(): pl.pallas_call(functools.partial(kernel, cfg), out_shape=shapes, in_specs...  78 us
    pallas_call x1, Pallas kernels, shards(): pl.pallas_call(placing, out_shape=shapes, in_specs=[any_space] * 2, out_s...  1.89 us

profile of v5, /device:TPU:1, one launch (start us, length us, event | category | flops | bytes accessed | tf_op | source)
XLA Modules:
  0.0 80.5 jit_solution(3441267511874013680)
XLA Ops:
  0.6 78.0 %shard_map.86 = (bf16[64,3584]{1,0:T(8,128)(2,1)}, bf16[64,1024]{1,0:T(8,128)(2,1)}) custom-call(s32[8,9]{1,0:T(8,128)} %owner_ref.1, bf16[128,3584]{1,0:T(8,128)(2,1)} %hid_hbm.1, bf16[128,1024]{1,0:T(8,128)(2,1)} %cot_hbm.1, bf16[64,3584]{1,0:T(8,128)(2,1)} %bitcast.2, bf16[64,1024]{1,0:T(8,128)(2,1)} %up_hbm.1, f32[2,512,512]{2,1,0:T(8,128)} %left_hbm.1, ...), custom_call_target="tpu_custom_call" | custom-call | tf_op jit(solution)/shard_map/pallas_call | solution.py:476
  78.6 1.9 %shard_map.87 = (bf16[64,3584]{1,0:T(8,128)(2,1)}, bf16[64,1024]{1,0:T(8,128)(2,1)}) custom-call(bf16[64,3584]{1,0:T(8,128)(2,1)} %get-tuple-element.6.first_in, bf16[64,1024]{1,0:T(8,128)(2,1)} %get-tuple-element.7.second_in), custom_call_target="tpu_custom_call" | custom-call | tf_op jit(solution)/shard_map/pallas_call | solution.py:527
